TPU v7x, 32 devices: a whole 2x2x4 slice. The times are simulated.
32 devices in a mesh: ctx: 8 (over z, core), tp: 2 (over x), run: 2 (over y).
Axes of the slice: x: 2, y: 2, z: 4, core: 2. Of those that a mesh axis runs over, the one named last changes fastest.
Arguments:
- tokens: bfloat16 [4096, 5120], P(('run', 'ctx')), parts along dimension 0, may hold values from -28 to 28
- block_order: int32 [32], replicated, may hold values from 0 to 31, each once
- doc_lengths: int32 [16], replicated, may hold values from 1 to 512, 2048 in all
- patch_pos: int32 [512], P(('run', 'ctx')), parts along dimension 0, may hold values from 0 to 2047, as said below
- clean_rows: bfloat16 [512, 5120], P(('run', 'ctx')), parts along dimension 0, may hold values from -6 to 6
- w_query: bfloat16 [5120, 5120], P(None, 'tp'), may hold values from -0.078125 to 0.078125
- q_bias: bfloat16 [5120], P('tp'), may hold values from -3 to 3
- w_key: bfloat16 [5120, 1024], P(None, 'tp'), may hold values from -0.078125 to 0.078125
- k_bias: bfloat16 [1024], P('tp'), may hold values from -3 to 3
- w_value: bfloat16 [5120, 1024], P(None, 'tp'), may hold values from -0.078125 to 0.078125
- v_bias: bfloat16 [1024], P('tp'), may hold values from -3 to 3
Outputs:
- attended: bfloat16 [4096, 5120], P(('run', 'ctx'), 'tp'), parts along dimension 0
There are 2 independent parts, one for each index of `run`. A program takes and returns all parts, laid end to end along the dimension named above; an argument that names none is the same for every part. Nothing has to cross between parts.
Inputs may be any that keep to these rules, and one draw needn't show every extreme that they name: `block_order`: every block index appears exactly once. `doc_lengths`: the lengths sum to 2048 and the largest equals 512. `patch_pos`: the 256 positions are distinct positions of the sequence, the first and the last position among them.
All inputs are finite; a program needn't handle non-finite values.
Results may differ from a plain program's by a relative error of at most 0.0076.
Values may be sent and summed in bfloat16 or wider, within the bound.
A program may use at most 128 MiB of HBM per device.

v0:
```python
import functools

import jax
import jax.numpy as jnp
import numpy as np
from jax import lax
from jax.experimental import pallas as pl
from jax.experimental.pallas import tpu as pltpu
from jax.sharding import PartitionSpec as P

HD = 128
BLOCK = 64
THETA = 1000000.0
CUTS = 2
MESH = pl.DeviceIdType.MESH


def block_places(block, length_ref):
    place = block * BLOCK + lax.broadcasted_iota(jnp.int32, (BLOCK, HD), 0)
    start = jnp.zeros((BLOCK, HD), jnp.int32)
    bound = jnp.int32(0)
    for j in range(length_ref.shape[0]):
        bound = bound + length_ref[j]
        start = jnp.where(place >= bound, bound, start)
    return place, start


def project_kernel(
    n,
    tp,
    order_ref,
    length_ref,
    patch_ref,
    freq_ref,
    bias_ref,
    tok_hbm,
    clean_hbm,
    wq_hbm,
    wk_hbm,
    wv_hbm,
    q_hbm,
    k_out,
    v_out,
    place_ref,
    cos_ref,
    sin_ref,
    pos_ref,
    q_out,
    tok,
    clean,
    wq,
    wk,
    wv,
    rows,
    posbuf,
    k_own,
    v_own,
    load_sem,
    zs,
    zr,
    ts,
    tr,
    cs,
    cr,
    ps,
    pr,
    kzs,
    kzr,
    kcs,
    kcr,
    own_sem,
):
    me = lax.axis_index("ctx")
    mine = lax.axis_index("tp")
    nz = n // 2
    z, c = me // 2, lax.rem(me, 2)
    right = lax.rem(z + 1, nz) * 2 + c
    left = lax.rem(z + nz - 1, nz) * 2 + c
    sib = z * 2 + 1 - c
    local, depth = tok.shape
    each = clean_hbm.shape[0]
    half = each // 2
    width = depth // tp
    kvw = wk.shape[1]
    qw = wq.shape[1]
    steps = nz - 1

    loads = [
        pltpu.make_async_copy(clean_hbm, rows.at[pl.ds(pl.multiple_of(me * each, each), each), :], load_sem.at[0]),
        pltpu.make_async_copy(tok_hbm, tok, load_sem.at[1]),
        pltpu.make_async_copy(wk_hbm, wk, load_sem.at[2]),
        pltpu.make_async_copy(wv_hbm, wv, load_sem.at[3]),
        pltpu.make_async_copy(wq_hbm, wq, load_sem.at[4]),
        pltpu.make_async_copy(clean_hbm, clean, load_sem.at[5]),
    ]
    loads[5].start()
    for load in loads[:5]:
        load.start()

    barrier = pltpu.get_barrier_semaphore()
    for k in range(1, n):
        pl.semaphore_signal(barrier, inc=1, device_id={"ctx": lax.rem(me + k, n)}, device_id_type=MESH)
    for k in range(1, tp):
        pl.semaphore_signal(barrier, inc=1, device_id={"tp": lax.rem(mine + k, tp)}, device_id_type=MESH)
    pl.semaphore_wait(barrier, n - 1 + tp - 1)

    def remote(src, dst, send, recv, where):
        return pltpu.make_async_remote_copy(
            src_ref=src, dst_ref=dst, send_sem=send, recv_sem=recv, device_id=where, device_id_type=MESH
        )

    started = []

    def go(copy):
        copy.start()
        started.append(copy)
        return copy

    own_columns = pl.ds(pl.multiple_of(mine * width, 128), width)

    def source(d, s):
        return lax.rem(z - s + nz, nz) * 2 + c if d == 0 else lax.rem(z + s, nz) * 2 + c

    def piece(block, d):
        return pl.ds(pl.multiple_of(block * each + d * half, half), half)

    lane = lax.broadcasted_iota(jnp.int32, pos_ref.shape, 1)

    def put(j, row):
        return jnp.where(lane == me * each + j, patch_ref[j], row)

    pos_ref[...] = lax.fori_loop(0, each, put, jnp.full(pos_ref.shape, -1, jnp.int32))
    loads[5].wait()
    for d in range(2):
        go(
            remote(
                clean.at[pl.ds(d * half, half), own_columns],
                rows.at[piece(me, d), own_columns],
                zs.at[d * steps],
                zr.at[d * steps],
                {"ctx": right if d == 0 else left},
            )
        )
    for k in range(1, n):
        go(remote(pos_ref, posbuf.at[me], ps.at[k - 1], pr.at[k - 1], {"ctx": lax.rem(me + k, n)}))
    own_core = go(
        remote(clean, rows.at[pl.ds(pl.multiple_of(me * each, each), each), :], cs.at[2 * steps], cr.at[2 * steps], {"ctx": sib})
    )
    posbuf[me] = pos_ref[...]

    first_half = lax.broadcasted_iota(jnp.int32, (BLOCK, HD), 1) < HD // 2
    for b in range(local // BLOCK):
        place, start = block_places(order_ref[me * (local // BLOCK) + b], length_ref)
        angles = (place - start).astype(jnp.float32) * freq_ref[...]
        here = pl.ds(b * BLOCK, BLOCK)
        place_ref[here, :] = place
        cos_ref[here, :] = jnp.cos(angles)
        sines = jnp.sin(angles)
        sin_ref[here, :] = jnp.where(first_half, -sines, sines)

    core_copies = []

    def to_core(s):
        for d in range(2):
            region = rows.at[piece(source(d, s + 1), d), :]
            for k in range(1, tp):
                at = (d * steps + s) * (tp - 1) + k - 1
                part = rows.at[
                    piece(source(d, s + 1), d),
                    pl.ds(pl.multiple_of(lax.rem(mine + tp - k, tp) * width, 128), width),
                ]
                remote(part, part, ts.at[at], tr.at[at], {"tp": lax.rem(mine + k, tp)}).wait_recv()
            core_copies.append(go(remote(region, region, cs.at[d * steps + s], cr.at[d * steps + s], {"ctx": sib})))

    for s in range(steps):
        for d in range(2):
            part = rows.at[piece(source(d, s + 1), d), own_columns]
            where = {"ctx": right if d == 0 else left}
            at = d * steps + s
            remote(part, part, zs.at[at], zr.at[at], where).wait_recv()
            if s < steps - 1:
                go(remote(part, part, zs.at[at + 1], zr.at[at + 1], where))
            for k in range(1, tp):
                to = at * (tp - 1) + k - 1
                go(remote(part, part, ts.at[to], tr.at[to], {"tp": lax.rem(mine + k, tp)}))
        if s > 0:
            to_core(s - 1)
    to_core(steps - 1)
    own_core.wait_recv()
    for copy in core_copies:
        copy.wait_recv()
    for k in range(1, n):
        remote(pos_ref, posbuf.at[me], ps.at[k - 1], pr.at[k - 1], {"ctx": me}).wait_recv()
    loads[0].wait()
    loads[1].wait()

    everyone = jnp.max(posbuf[...], axis=0)[0:1, :]
    hits = place_ref[:, 0:1] == everyone
    chosen = jnp.where(hits, 1.0, 0.0).astype(jnp.bfloat16)
    present = jnp.max(jnp.where(hits, 1.0, 0.0), axis=1, keepdims=True) > 0.5
    span = 512

    def patch(j, carry):
        columns = pl.ds(pl.multiple_of(j * span, span), span)
        picked = jnp.dot(chosen, rows[:, columns], preferred_element_type=jnp.float32)
        tok[:, columns] = jnp.where(present, picked, tok[:, columns].astype(jnp.float32)).astype(jnp.bfloat16)
        return carry

    lax.fori_loop(0, depth // span, patch, 0)

    def project(weight, base, out, rotated, share=0, shares=1):
        total = weight.shape[1]
        tile = 256 if total % 256 == 0 else 128

        def one(j, carry):
            columns = pl.ds(pl.multiple_of(j * tile, tile), tile)
            result = jnp.dot(tok[...], weight[:, columns], preferred_element_type=jnp.float32)
            result = result + bias_ref[:, pl.ds(pl.multiple_of(base + j * tile, HD), tile)]
            if rotated:
                parts = []
                for h in range(tile // HD):
                    head = result[:, h * HD : (h + 1) * HD]
                    parts.append(head * cos_ref[...] + pltpu.roll(head, HD // 2, 1) * sin_ref[...])
                result = jnp.concatenate(parts, axis=1) if len(parts) > 1 else parts[0]
            out[:, columns] = result.astype(jnp.bfloat16)
            return carry

        tiles = total // tile
        lax.fori_loop(share * tiles // shares, (share + 1) * tiles // shares, one, 0)

    cut = local // CUTS

    def slot(block, h):
        return pl.ds(pl.multiple_of(block * local + h * cut, cut), cut)

    def sem_at(d, s, h):
        return (d * nz + s) * CUTS + h

    outs = (k_out, v_out)
    owns = (k_own, v_own)
    own_copies = []

    def send_own(d):
        where = {"ctx": right if d == 0 else left}
        for h in range(CUTS):
            src = owns[d].at[pl.ds(h * cut, cut), :]
            dst = outs[d].at[slot(me, h), :]
            at = sem_at(d, 0, h)
            go(remote(src, dst, kzs.at[at], kzr.at[at], where))
        for h in range(CUTS):
            src = owns[d].at[pl.ds(h * cut, cut), :]
            dst = outs[d].at[slot(me, h), :]
            at = sem_at(d, steps, h)
            go(remote(src, dst, kcs.at[at], kcr.at[at], {"ctx": sib}))
        copy = pltpu.make_async_copy(owns[d], outs[d].at[pl.ds(pl.multiple_of(me * local, local), local), :], own_sem.at[d])
        copy.start()
        own_copies.append(copy)

    loads[2].wait()
    project(wk, qw, k_own, True)
    send_own(0)
    loads[3].wait()
    project(wv, qw + kvw, v_own, False)
    send_own(1)
    loads[4].wait()

    def pass_on(s, h):
        for d in range(2):
            where = {"ctx": right if d == 0 else left}
            part = outs[d].at[slot(source(d, s + 1), h), :]
            at = sem_at(d, s, h)
            remote(part, part, kzs.at[at], kzr.at[at], where).wait_recv()
            if s < steps - 1:
                then = sem_at(d, s + 1, h)
                go(remote(part, part, kzs.at[then], kzr.at[then], where))
            go(remote(part, part, kcs.at[at], kcr.at[at], {"ctx": sib}))

    pieces = [(s, h) for s in range(steps) for h in range(CUTS)]
    for share in range(CUTS + 1):
        project(wq, 0, q_out, True, share, CUTS + 1)
        if share < CUTS:
            pass_on(*pieces[share])
    q_copy = pltpu.make_async_copy(q_out, q_hbm, own_sem.at[2])
    q_copy.start()
    own_copies.append(q_copy)
    for step_and_cut in pieces[CUTS:]:
        pass_on(*step_and_cut)
    for s in range(nz):
        for h in range(CUTS):
            for d in range(2):
                at = sem_at(d, s, h)
                part = outs[d].at[slot(source(d, lax.rem(s + 1, nz)) + 1 - 2 * c, h), :]
                remote(part, part, kcs.at[at], kcr.at[at], {"ctx": sib}).wait_recv()
    for copy in own_copies:
        copy.wait()
    for copy in started:
        copy.wait_send()


def attend_kernel(kvh, group, order_ref, length_ref, q_ref, k_ref, v_ref, out_ref, inv, qs, m_s, l_s, acc_s):
    i = pl.program_id(0)
    wide = 4
    keys = wide * BLOCK
    base = lax.axis_index("ctx") * pl.num_programs(0)

    @pl.when(i == 0)
    def _():
        def put(j, carry):
            inv[order_ref[j]] = j
            return carry

        lax.fori_loop(0, order_ref.shape[0], put, 0)

    mine = order_ref[base + i]
    bound = jnp.int32(0)
    first_start = jnp.int32(0)
    for j in range(length_ref.shape[0]):
        bound = bound + length_ref[j]
        first_start = jnp.where(mine * BLOCK >= bound, bound, first_start)
    low = first_start // BLOCK
    for h in range(kvh):
        for g in range(group):
            head = h * group + g
            qs[h, g * BLOCK : (g + 1) * BLOCK, :] = q_ref[:, head * HD : (head + 1) * HD]
    m_s[...] = jnp.full_like(m_s, -1e30)
    l_s[...] = jnp.zeros_like(l_s)
    acc_s[...] = jnp.zeros_like(acc_s)
    places, starts = block_places(mine, length_ref)
    exponent = HD**-0.5 * 1.4426950408889634

    def step(t, carry):
        first = mine - wide * t - (wide - 1)
        at = [inv[jnp.maximum(first + w, 0)] for w in range(wide)]
        at = [pl.multiple_of(a * BLOCK, BLOCK) for a in at]
        lanes = first * BLOCK + lax.broadcasted_iota(jnp.int32, (BLOCK, HD), 1)
        bias = []
        for w in range(keys // HD):
            shown = (lanes + w * HD >= starts) & (lanes + w * HD <= places)
            bias.append(jnp.where(shown, 0.0, -1e30))
        bias = jnp.concatenate([jnp.concatenate(bias, axis=1)] * group, axis=0)
        for h in range(kvh):
            head = slice(h * HD, (h + 1) * HD)
            k = jnp.concatenate([k_ref[pl.ds(a, BLOCK), head] for a in at], axis=0)
            v = jnp.concatenate([v_ref[pl.ds(a, BLOCK), head] for a in at], axis=0)
            scores = bias + lax.dot_general(
                qs[h], k, (((1,), (1,)), ((), ())), preferred_element_type=jnp.float32
            )
            old = m_s[h]
            new = jnp.maximum(old, jnp.max(scores, axis=1, keepdims=True))
            factor = jnp.exp2((old - new) * exponent)
            weights = jnp.exp2((scores - jnp.concatenate([new] * (keys // HD), axis=1)) * exponent)
            m_s[h] = new
            total = weights[:, :HD]
            for w in range(1, keys // HD):
                total = total + weights[:, w * HD : (w + 1) * HD]
            l_s[h] = l_s[h] * factor + total
            acc_s[h] = acc_s[h] * factor + jnp.dot(
                weights.astype(jnp.bfloat16), v, preferred_element_type=jnp.float32
            )
        return carry

    lax.fori_loop(0, (mine - low + wide) // wide, step, 0)
    for h in range(kvh):
        result = (acc_s[h] / jnp.sum(l_s[h], axis=1, keepdims=True)).astype(jnp.bfloat16)
        for g in range(group):
            head = h * group + g
            out_ref[:, head * HD : (head + 1) * HD] = result[g * BLOCK : (g + 1) * BLOCK, :]


def body(n, tp, tokens, block_order, doc_lengths, patch_pos, clean_rows, w_query, q_bias, w_key, k_bias, w_value, v_bias):
    local, depth = tokens.shape
    each = patch_pos.shape[0]
    patches = each * n
    qw, kvw = w_query.shape[1], w_key.shape[1]
    kvh = kvw // HD
    group = qw // kvw
    blocks = local // BLOCK
    nz = n // 2
    halves = np.float64(THETA) ** (-2.0 * np.arange(HD // 2) / HD)
    frequency = jnp.asarray(np.concatenate([halves, halves])[None, :].astype(np.float32))
    bias = lax.optimization_barrier(
        jnp.concatenate([q_bias.astype(jnp.float32), k_bias.astype(jnp.float32), v_bias.astype(jnp.float32)])
    )[None, :]

    smem = pl.BlockSpec(memory_space=pltpu.SMEM)
    vmem = pl.BlockSpec(memory_space=pltpu.VMEM)
    hbm = pl.BlockSpec(memory_space=pl.ANY)
    dma = pltpu.SemaphoreType.DMA
    steps = nz - 1
    query, keys, values = pl.pallas_call(
        functools.partial(project_kernel, n, tp),
        out_shape=(
            jax.ShapeDtypeStruct((local, qw), jnp.bfloat16),
            jax.ShapeDtypeStruct((n * local, kvw), jnp.bfloat16),
            jax.ShapeDtypeStruct((n * local, kvw), jnp.bfloat16),
        ),
        in_specs=[smem] * 3 + [vmem] * 2 + [hbm] * 5,
        out_specs=(hbm, hbm, hbm),
        scratch_shapes=[
            pltpu.VMEM((local, HD), jnp.int32),
            pltpu.VMEM((local, HD), jnp.float32),
            pltpu.VMEM((local, HD), jnp.float32),
            pltpu.VMEM((8, patches), jnp.int32),
            pltpu.VMEM((local, qw), jnp.bfloat16),
            pltpu.VMEM((local, depth), jnp.bfloat16),
            pltpu.VMEM((each, depth), jnp.bfloat16),
            pltpu.VMEM((depth, qw), jnp.bfloat16),
            pltpu.VMEM((depth, kvw), jnp.bfloat16),
            pltpu.VMEM((depth, kvw), jnp.bfloat16),
            pltpu.VMEM((patches, depth), jnp.bfloat16),
            pltpu.VMEM((n, 8, patches), jnp.int32),
            pltpu.VMEM((local, kvw), jnp.bfloat16),
            pltpu.VMEM((local, kvw), jnp.bfloat16),
            dma((6,)),
            dma((2 * steps,)),
            dma((2 * steps,)),
            dma((2 * steps * (tp - 1),)),
            dma((2 * steps * (tp - 1),)),
            dma((2 * steps + 1,)),
            dma((2 * steps + 1,)),
            dma((n - 1,)),
            dma((n - 1,)),
            dma((2 * nz * CUTS,)),
            dma((2 * nz * CUTS,)),
            dma((2 * nz * CUTS,)),
            dma((2 * nz * CUTS,)),
            dma((3,)),
        ],
        compiler_params=pltpu.CompilerParams(
            collective_id=0, has_side_effects=True, vmem_limit_bytes=58 * 1024 * 1024
        ),
        cost_estimate=pl.CostEstimate(
            flops=2 * local * depth * (qw + 2 * kvw), bytes_accessed=2 * depth * (qw + 2 * kvw), transcendentals=0
        ),
    )(
        block_order,
        doc_lengths,
        patch_pos,
        frequency,
        bias,
        tokens,
        clean_rows,
        w_query,
        w_key,
        w_value,
    )

    whole = lambda i, *_: (0, 0)
    part = lambda i, *_: (i, 0)
    return pl.pallas_call(
        functools.partial(attend_kernel, kvh, group),
        out_shape=jax.ShapeDtypeStruct((local, qw), jnp.bfloat16),
        grid_spec=pltpu.PrefetchScalarGridSpec(
            num_scalar_prefetch=2,
            grid=(blocks,),
            in_specs=[
                pl.BlockSpec((BLOCK, qw), part),
                pl.BlockSpec((n * local, kvw), whole),
                pl.BlockSpec((n * local, kvw), whole),
            ],
            out_specs=pl.BlockSpec((BLOCK, qw), part),
            scratch_shapes=[
                pltpu.SMEM((n * local // BLOCK,), jnp.int32),
                pltpu.VMEM((kvh, group * BLOCK, HD), jnp.bfloat16),
                pltpu.VMEM((kvh, group * BLOCK, HD), jnp.float32),
                pltpu.VMEM((kvh, group * BLOCK, HD), jnp.float32),
                pltpu.VMEM((kvh, group * BLOCK, HD), jnp.float32),
            ],
        ),
        compiler_params=pltpu.CompilerParams(vmem_limit_bytes=60 * 1024 * 1024),
        cost_estimate=pl.CostEstimate(flops=10**9, bytes_accessed=6 * 10**6, transcendentals=10**6),
    )(block_order, doc_lengths, query, keys, values)


def solution(mesh):
    in_specs = (
        P(("run", "ctx"), None),
        P(),
        P(),
        P(("run", "ctx")),
        P(("run", "ctx"), None),
        P(None, "tp"),
        P("tp"),
        P(None, "tp"),
        P("tp"),
        P(None, "tp"),
        P("tp"),
    )
    out_specs = P(("run", "ctx"), "tp")
    return jax.shard_map(
        functools.partial(body, mesh.shape["ctx"], mesh.shape["tp"]),
        mesh=mesh,
        in_specs=in_specs,
        out_specs=out_specs,
        check_vma=False,
    )
```

profile of v0, /device:TPU:1, one launch (start us, length us, event | category | flops | bytes accessed | tf_op | source)
XLA Modules:
  0.0 82.2 jit_solution(2455175050831513427)
XLA Ops:
  0.0 0.7 maximum_convert_fusion
  0.7 0.6 broadcast_in_dim.3.bias_ref
  1.3 69.1 %shard_map.118 = (bf16[256,2560]{1,0:T(8,128)(2,1)}, bf16[2048,512]{1,0:T(8,128)(2,1)}, bf16[2048,512]{1,0:T(8,128)(2,1)}) custom-call(s32[32]{0:T(128)} %order_ref.3, s32[16]{0:T(128)} %length_ref.3, s32[32]{0:T(128)} %patch_ref.1, f32[1,128]{1,0:T(1,128)} %constant.2.clone.freq_ref, f32[1,3584]{1,0:T(1,128)} %broadcast_in_dim.3.bias_ref, ...), custom_call_target="tpu_custom_call" | custom-call | flops 9395240960 | bytes 36700160 | tf_op jit(solution)/shard_map/pallas_call | solution.py:390
  70.5 11.7 %shard_map.119 = bf16[256,2560]{1,0:T(8,128)(2,1)} custom-call(s32[32]{0:T(128)} %order_ref.3, s32[16]{0:T(128)} %length_ref.3, bf16[256,2560]{1,0:T(8,128)(2,1)} %get-tuple-element.8.q_ref, bf16[2048,512]{1,0:T(8,128)(2,1)} %get-tuple-element.9.k_ref, bf16[2048,512]{1,0:T(8,128)(2,1)} %get-tuple-element.10.v_ref), custom_call_target="tpu_custom_call" | custom-call | flops 1000000000 | bytes 6000000 | tf_op jit(solution)/shard_map/pallas_call | solution.py:450
where the time goes:
time: 81.3 us; the launch traced here: 82.2 us
  Pallas kernels  80.8 us (99%)
    pallas_call x1, Pallas kernels, body(): pl.pallas_call(functools.partial(project_kernel, n, tp), out_shape=(jax.S...  69.1 us
    pallas_call x1, Pallas kernels, body(): pl.pallas_call(functools.partial(attend_kernel, kvh, group), out_shape=ja...  11.7 us

commit v1 on v0

--- a/solution.py
+++ b/solution.py
@@ -11,7 +11,7 @@
 HD = 128
 BLOCK = 64
 THETA = 1000000.0
-CUTS = 2
+CUTS = 4
 MESH = pl.DeviceIdType.MESH
 
 

time: 81.3 us -> 80.6 us (level); the launches traced: 82.2 us -> 79.4 us
  Pallas kernels: 80.8 us -> 78.1 us
    pallas_call x1, Pallas kernels: 11.7 us -> 8.68 us  [body(): pl.pallas_call(functools.partial(attend_kernel, kvh, group), out_shape=ja...]
where the time goes in v1:
time: 80.6 us; the launch traced here: 79.4 us
  Pallas kernels  78.1 us (97%)
    pallas_call x1, Pallas kernels, body(): pl.pallas_call(functools.partial(project_kernel, n, tp), out_shape=(jax.S...  69.4 us
    pallas_call x1, Pallas kernels, body(): pl.pallas_call(functools.partial(attend_kernel, kvh, group), out_shape=ja...  8.68 us

profile of v1, /device:TPU:1, one launch (start us, length us, event | category | flops | bytes accessed | tf_op | source)
XLA Modules:
  0.0 79.4 jit_solution(1697502213333961209)
XLA Ops:
  0.0 0.7 maximum_convert_fusion
  0.7 0.6 broadcast_in_dim.3.bias_ref
  1.3 69.4 %shard_map.118 = (bf16[256,2560]{1,0:T(8,128)(2,1)}, bf16[2048,512]{1,0:T(8,128)(2,1)}, bf16[2048,512]{1,0:T(8,128)(2,1)}) custom-call(s32[32]{0:T(128)} %order_ref.3, s32[16]{0:T(128)} %length_ref.3, s32[32]{0:T(128)} %patch_ref.1, f32[1,128]{1,0:T(1,128)} %constant.2.clone.freq_ref, f32[1,3584]{1,0:T(1,128)} %broadcast_in_dim.3.bias_ref, ...), custom_call_target="tpu_custom_call" | custom-call | flops 9395240960 | bytes 36700160 | tf_op jit(solution)/shard_map/pallas_call | solution.py:390
  70.8 8.7 %shard_map.119 = bf16[256,2560]{1,0:T(8,128)(2,1)} custom-call(s32[32]{0:T(128)} %order_ref.3, s32[16]{0:T(128)} %length_ref.3, bf16[256,2560]{1,0:T(8,128)(2,1)} %get-tuple-element.8.q_ref, bf16[2048,512]{1,0:T(8,128)(2,1)} %get-tuple-element.9.k_ref, bf16[2048,512]{1,0:T(8,128)(2,1)} %get-tuple-element.10.v_ref), custom_call_target="tpu_custom_call" | custom-call | flops 1000000000 | bytes 6000000 | tf_op jit(solution)/shard_map/pallas_call | solution.py:450
